TPU v7x, 128 devices: a whole 4x4x4 slice. The times are simulated.
128 devices in a mesh: fsdp: 16 (over y_lo, z, core), tp: 8 (over x, y_hi).
Axes of the slice: x: 4, y: 4 (y_hi: 2, y_lo: 2; y = y_hi * 2 + y_lo), z: 4, core: 2. Of those that a mesh axis runs over, the one named last changes fastest.
Arguments:
- hidden_in: bfloat16 [1024, 4096], P('fsdp'), may hold values from -3 to 3
- queries: bfloat16 [2, 1024, 8192], P(None, ('fsdp', 'tp')), may hold values from -170 to 170
- key_cache: bfloat16 [1024, 256, 512], P(('fsdp', 'tp')), may hold values from -6 to 6
- value_cache: bfloat16 [1024, 256, 512], P(('fsdp', 'tp')), may hold values from -6 to 6
- new_keys: bfloat16 [2, 1024, 512], P(None, ('fsdp', 'tp')), may hold values from -6 to 6
- new_values: bfloat16 [2, 1024, 512], P(None, ('fsdp', 'tp')), may hold values from -6 to 6
- lengths: int32 [1024], P(('fsdp', 'tp')), may hold values from 2 to 256
- routes: int32 [2, 1024, 8], P(None, 'fsdp'), may hold values from 0 to 127, all different within a row; in each aligned block of 64 rows (0 to 63, 64 to 127, ..., all dimensions but the last counted through in order) at most 8 rows name the same one
- route_weights: float32 [2, 1024, 8], P(None, 'fsdp'), may hold values from 0.05 to 1
- norm_gain: float32 [4096], replicated, may hold values from 0.1 to 1.9
- gate_master: float32 [8, 1536, 4096], P(None, ('fsdp', 'tp')), may hold values from -0.09375 to 0.09375
- up_master: float32 [8, 1536, 4096], P(None, ('fsdp', 'tp')), may hold values from -0.09375 to 0.09375
- down_master: float32 [8, 1536, 4096], P(None, ('fsdp', 'tp')), may hold values from -0.3125 to 0.3125
- out_proj: bfloat16 [8192, 4096], P('tp'), may hold values from -0.0625 to 0.0625
Outputs:
- hidden_out: bfloat16 [1024, 4096], P('fsdp', 'tp')
- scale_log2: float32 [3, 8, 12, 32], replicated
Inputs may be any that keep to these rules, and one draw needn't show every extreme that they name: `routes`: within one step and one index of fsdp (aligned blocks of 64 rows), no expert is named by more than 8 rows.
All inputs are finite; a program needn't handle non-finite values.
Results may differ from a plain program's by a relative error of at most 0.0095.
Values may be sent and summed in bfloat16 or wider, within the bound.
A program may use at most 256 MiB of HBM per device.

v0:
```python
import jax
import jax.numpy as jnp
from jax import lax
from jax.sharding import PartitionSpec as P

D = 4096
FF = 1536
QH = 64
KVH = 4
HD = 128
BLOCK = 128
WIN = 8
CAP = 8
neg_fill = -1e30
epsilon = 1e-06
fp_limit = 448.0
grid_floor = 2.0 ** (-10)
least_exponent = -6.0


def cut_along(array, dim, peers):
    before, after = (array.shape[:dim], array.shape[dim + 1 :])
    return jnp.moveaxis(array.reshape(*before, peers, -1, *after), dim, 0)


def sent_and_summed(array, axis, dim):
    blocks = cut_along(array, dim, lax.axis_size(axis))
    arrived = lax.all_to_all(blocks, axis, split_axis=0, concat_axis=0, tiled=True)
    return arrived.astype(jnp.float32).sum(axis=0)


def copy_for_each(array, axis):
    peers = lax.axis_size(axis)
    return lax.all_to_all(
        jnp.broadcast_to(array[None], (peers, *array.shape)), axis, 0, 0, tiled=True
    )


def joined_along(blocks, dim):
    blocks = jnp.moveaxis(blocks, 0, dim)
    lengths = blocks.shape
    return blocks.reshape(*lengths[:dim], lengths[dim] * lengths[dim + 1], *lengths[dim + 2 :])


def collect(array, axis, dim):
    blocks = copy_for_each(array, axis)
    return joined_along(blocks, dim)


def grid_round(values):
    magnitude = jnp.abs(values)
    exponent = jnp.maximum(jnp.floor(jnp.log2(jnp.maximum(magnitude, grid_floor))), least_exponent)
    spacing = jnp.exp2(exponent - 3.0)
    return jnp.sign(values) * jnp.floor(magnitude / spacing + 0.5) * spacing


def attention_rows(queries_now, cache_keys, cache_values, fresh_keys, fresh_values, lengths):
    row_count = queries_now.shape[0]
    positions = cache_keys.shape[1]
    group = QH // KVH
    score_scale = HD ** (-0.5)
    fresh_count = fresh_keys.shape[0]
    query_heads = queries_now.reshape(row_count, KVH, group, HD)
    key_heads = cache_keys.reshape(row_count, positions, KVH, HD)
    value_heads = cache_values.reshape(row_count, positions, KVH, HD)
    fresh_key_heads = fresh_keys.reshape(fresh_count, row_count, KVH, HD)
    fresh_value_heads = fresh_values.reshape(fresh_count, row_count, KVH, HD)
    cached_scores = (
        jnp.einsum("rkgd,rpkd->rkgp", query_heads, key_heads, preferred_element_type=jnp.float32)
        * score_scale
    )
    fresh_scores = (
        jnp.einsum(
            "rkgd,srkd->rkgs", query_heads, fresh_key_heads, preferred_element_type=jnp.float32
        )
        * score_scale
    )
    alive_mask = (jnp.arange(positions, dtype=jnp.int32)[None, :] < lengths[:, None])[
        :, None, None, :
    ]
    peak_score = jnp.maximum(
        jnp.max(jnp.where(alive_mask, cached_scores, neg_fill), axis=-1),
        jnp.max(fresh_scores, axis=-1),
    )
    cached_weights = jnp.where(alive_mask, jnp.exp(cached_scores - peak_score[..., None]), 0.0)
    fresh_weights = jnp.exp(fresh_scores - peak_score[..., None])
    weight_sum = jnp.sum(cached_weights, axis=-1) + jnp.sum(fresh_weights, axis=-1)
    cached_probs = (cached_weights / weight_sum[..., None]).astype(jnp.bfloat16)
    fresh_probs = (fresh_weights / weight_sum[..., None]).astype(jnp.bfloat16)
    output = jnp.einsum(
        "rkgp,rpkd->rkgd", cached_probs, value_heads, preferred_element_type=jnp.float32
    )
    output = output + jnp.einsum(
        "rkgs,srkd->rkgd", fresh_probs, fresh_value_heads, preferred_element_type=jnp.float32
    )
    return output.astype(jnp.bfloat16).reshape(row_count, QH * HD)


def routing_tables(routes, route_weights):
    rows = routes.shape[0]
    weight_sum = jnp.sum(route_weights, axis=1)
    experts = jnp.arange(WIN, dtype=jnp.int32)
    matches = routes[None, :, :] == experts[:, None, None]
    chosen = jnp.any(matches, axis=2)
    gate_share = (
        jnp.sum(jnp.where(matches, route_weights[None, :, :], 0.0), axis=2) / weight_sum[None, :]
    )
    earlier = jnp.arange(rows)[:, None] < jnp.arange(rows)[None, :]
    slot_index = jnp.sum(jnp.where(earlier[None], chosen.astype(jnp.int32)[:, :, None], 0), axis=1)
    places = jnp.arange(CAP, dtype=jnp.int32)
    picked = (slot_index[:, None, :] == places[None, :, None]) & chosen[:, None, :]
    slot_share = jnp.sum(jnp.where(picked, gate_share[:, None, :], 0.0), axis=2)
    return (picked.astype(jnp.bfloat16), slot_share)


def block_maxima(masters, fsdp_pos, tp_pos, tp_count):
    shard_rows = masters.shape[2]
    magnitude = jnp.max(jnp.abs(masters).reshape(3, WIN, shard_rows, D // BLOCK, BLOCK), axis=4)
    first_tile = fsdp_pos * shard_rows * tp_count // BLOCK
    owned = (fsdp_pos * tp_count + tp_pos) * shard_rows + jnp.arange(shard_rows, dtype=jnp.int32)
    second = owned // BLOCK - first_tile == 1
    mine = jnp.stack(
        [
            jnp.max(jnp.where(second[None, None, :, None], 0.0, magnitude), axis=2),
            jnp.max(jnp.where(second[None, None, :, None], magnitude, 0.0), axis=2),
        ]
    )
    group = jnp.max(copy_for_each(mine, "tp"), axis=0)
    every = copy_for_each(group, "fsdp")
    tiles = []
    for tile in range(FF // BLOCK):
        parts = []
        for owner in range(16):
            first = owner * 96 // BLOCK
            if first == tile:
                parts.append(every[owner, 0])
            if first + 1 == tile and owner * 96 + 95 >= tile * BLOCK:
                parts.append(every[owner, 1])
        tiles.append(jnp.max(jnp.stack(parts), axis=0))
    return (jnp.stack(tiles, axis=2), first_tile, second)


def local(
    hidden_in,
    queries,
    key_cache,
    value_cache,
    new_keys,
    new_values,
    lengths,
    routes,
    route_weights,
    norm_gain,
    gate_master,
    up_master,
    down_master,
    out_proj,
):
    tp_count = lax.axis_size("tp")
    fsdp_pos = lax.axis_index("fsdp")
    tp_pos = lax.axis_index("tp")
    shard_rows = gate_master.shape[1]
    masters = jnp.stack([gate_master, up_master, down_master])
    block_max, first_tile, second = block_maxima(masters, fsdp_pos, tp_pos, tp_count)
    scales = (block_max + epsilon) / fp_limit
    scale_log2 = jnp.log2(scales)
    near = lax.dynamic_slice_in_dim(scales, first_tile, 1, 2)
    far = lax.dynamic_slice_in_dim(scales, jnp.minimum(first_tile + 1, FF // BLOCK - 1), 1, 2)
    factors = jnp.where(second[None, None, :, None], far, near)[..., None]
    tiles = masters.reshape(3, WIN, shard_rows, D // BLOCK, BLOCK)
    quantized = grid_round(tiles / factors).astype(jnp.bfloat16).astype(jnp.float32)
    restored = (quantized * factors).astype(jnp.bfloat16).reshape(3, WIN, shard_rows, D)
    arrived = lax.all_to_all(
        restored.transpose(1, 0, 2, 3), "tp", split_axis=0, concat_axis=0, tiled=True
    )
    own = [arrived[:, i].reshape(tp_count * shard_rows, D) for i in range(3)]
    share_cols = D // tp_count
    own_start = tp_pos * share_cols
    current = lax.dynamic_slice_in_dim(hidden_in, own_start, share_cols, 1)
    tables = [routing_tables(routes[s], route_weights[s]) for s in range(2)]
    heads = jnp.stack(
        [
            attention_rows(
                queries[s], key_cache, value_cache, new_keys[: s + 1], new_values[: s + 1], lengths
            )
            for s in range(2)
        ]
    )
    regrouped = lax.all_to_all(heads, "tp", split_axis=2, concat_axis=1, tiled=True)
    projections = []
    for s in range(2):
        projected = jnp.dot(regrouped[s], out_proj, preferred_element_type=jnp.float32)
        projections.append(projected.astype(jnp.bfloat16))
    both = jnp.stack(projections)
    summed = sent_and_summed(both, "tp", 2)
    for s in range(2):
        picked, slot_share = tables[s]
        mixed = (current.astype(jnp.float32) + summed[s]).astype(jnp.bfloat16)
        slots = picked.reshape(WIN * CAP, -1)
        chosen = jnp.dot(slots, mixed, preferred_element_type=jnp.float32).astype(jnp.bfloat16)
        rows = collect_slots(chosen)
        values = rows.astype(jnp.float32)
        inverse = lax.rsqrt(jnp.mean(values * values, axis=1, keepdims=True) + epsilon)
        normed = (values * inverse * norm_gain[None, :]).astype(jnp.bfloat16)
        everyone = copy_for_each(normed, "fsdp").reshape(-1, D)
        gate = jnp.einsum("rd,hd->rh", everyone, own[0], preferred_element_type=jnp.float32)
        up = jnp.einsum("rd,hd->rh", everyone, own[1], preferred_element_type=jnp.float32)
        act = (jax.nn.silu(gate) * up).astype(jnp.bfloat16)
        partial = jnp.dot(act, own[2], preferred_element_type=jnp.float32).astype(jnp.bfloat16)
        output = sent_and_summed(partial, "fsdp", 0)
        share = lax.dynamic_slice_in_dim(slot_share, tp_pos, 1, 0)[0]
        weighted = (output * share[:, None]).astype(jnp.bfloat16)
        returned = lax.all_to_all(
            cut_along(weighted, 1, tp_count), "tp", split_axis=0, concat_axis=0, tiled=True
        ).reshape(WIN * CAP, share_cols)
        moe = lax.dot_general(
            slots, returned, (((0,), (0,)), ((), ())), preferred_element_type=jnp.float32
        )
        current = (mixed.astype(jnp.float32) + moe).astype(jnp.bfloat16)
    return (current, scale_log2)


def collect_slots(chosen):
    arrived = lax.all_to_all(chosen, "tp", split_axis=0, concat_axis=0, tiled=True)
    blocks = arrived.reshape(-1, CAP, chosen.shape[1])
    return joined_along(blocks, 1)


def solution(mesh):
    in_specs = (
        P("fsdp", None),
        P(None, ("fsdp", "tp"), None),
        P(("fsdp", "tp"), None, None),
        P(("fsdp", "tp"), None, None),
        P(None, ("fsdp", "tp"), None),
        P(None, ("fsdp", "tp"), None),
        P(("fsdp", "tp")),
        P(None, "fsdp", None),
        P(None, "fsdp", None),
        P(),
        P(None, ("fsdp", "tp"), None),
        P(None, ("fsdp", "tp"), None),
        P(None, ("fsdp", "tp"), None),
        P("tp", None),
    )
    out_specs = (P("fsdp", "tp"), P())
    return jax.shard_map(local, mesh=mesh, in_specs=in_specs, out_specs=out_specs, check_vma=False)
```

profile of v0, /device:TPU:0, one launch (start us, length us, event | category | flops | bytes accessed | tf_op | source)
XLA Modules:
  0.0 295.8 jit_solution(17559378506708630502)
XLA Ops:
  0.7 3.8 %fusion = f32[3,8,12,32]{1,3,2,0:T(8,128)S(1)} fusion(f32[1,8,12,32,128]{4,1,3,2,0:T(8,128)} %bitcast.259, f32[1,8,12,32,128]{4,1,3,2,0:T(8,128)} %bitcast.261, f32[1,8,12,32,128]{4,1,3,2,0:T(8,128)} %bitcast.263), kind=kLoop, calls=%fused_computation.4 | loop fusion | flops 4709376 | bytes 4755456 | tf_op jit(solution)/shard_map/reduce_max | solution.py:118
  5.7 7.0 %all-to-all-start.4 = ((f32[8,1,1536]{2,1,0:T(1,128)}), f32[8,1,1536]{2,1,0:T(1,128)S(1)}, u32[]{:S(2)}, u32[]{:S(2)}) async-start(f32[8,1,1536]{2,1,0:T(1,128)} %reshape.598), calls=%async_computation.4 | async-start | bytes 98304 | tf_op jit(solution)/shard_map/all_to_all | solution.py:34
  18.4 6.7 %copy.154 = bf16[2,8,8192]{1,0,2:T(2,128)(2,1)} copy(bf16[2,8,8192]{2,1,0:T(8,128)(2,1)S(1)} %pad_maximum_fusion) | data formatting | bytes 524288 | tf_op jit(solution)/shard_map/stack | solution.py:181
  25.1 6.4 %reshape.602 = bf16[8,2,8192]{2,1,0:T(2,128)(2,1)} reshape(bf16[8192,2,8]{2,1,0:T(2,128)(2,1)} %bitcast.257) | data formatting | bytes 524288
  33.9 5.5 %all-to-all-start.5 = ((f32[16,1,1536]{2,1,0:T(1,128)}), f32[16,1,1536]{2,1,0:T(1,128)S(1)}, u32[]{:S(2)}, u32[]{:S(2)}) async-start(f32[16,1,1536]{2,1,0:T(1,128)} %reshape.600), calls=%async_computation.5 | async-start | bytes 196608 | tf_op jit(solution)/shard_map/all_to_all | solution.py:34
  39.7 6.1 %all-to-all-done.5 = f32[16,1,1536]{2,1,0:T(1,128)S(1)} async-done(((f32[16,1,1536]{2,1,0:T(1,128)}), f32[16,1,1536]{2,1,0:T(1,128)S(1)}, u32[]{:S(2)}, u32[]{:S(2)}) %all-to-all-start.5) | async-done | bytes 98336 | tf_op jit(solution)/shard_map/all_to_all | solution.py:34
  45.8 7.8 %all-to-all-start = ((bf16[8,2,8192]{2,1,0:T(2,128)(2,1)}), bf16[8,2,8192]{2,1,0:T(2,128)(2,1)S(1)}, u32[]{:S(2)}, u32[]{:S(2)}) async-start(bf16[8,2,8192]{2,1,0:T(2,128)(2,1)} %reshape.602), calls=%async_computation | async-start | bytes 524288 | tf_op jit(solution)/shard_map/all_to_all | solution.py:189
  54.7 7.6 %all-to-all-done = bf16[8,2,8192]{2,1,0:T(2,128)(2,1)S(1)} async-done(((bf16[8,2,8192]{2,1,0:T(2,128)(2,1)}), bf16[8,2,8192]{2,1,0:T(2,128)(2,1)S(1)}, u32[]{:S(2)}, u32[]{:S(2)}) %all-to-all-start) | async-done | bytes 262176 | tf_op jit(solution)/shard_map/all_to_all | solution.py:189
  62.4 5.9 %reshape.603 = bf16[8192,2,8]{2,1,0:T(2,128)(2,1)} reshape(bf16[8,2,8192]{2,1,0:T(2,128)(2,1)S(1)} %all-to-all-done) | data formatting | bytes 524288
  68.3 5.9 %copy.169 = bf16[2,8,8,1024]{3,2,1,0:T(8,128)(2,1)S(1)} copy(bf16[2,8,8,1024]{1,0,3,2:T(2,128)(2,1)} %bitcast.258) | data formatting | bytes 524288 | tf_op jit(solution)/shard_map/all_to_all | solution.py:189
  74.3 4.9 %convolution_convert_fusion.2 = bf16[64,4096]{1,0:T(8,128)(2,1)S(1)} fusion(bf16[1024,4096]{1,0:T(8,128)(2,1)} %param.27, bf16[1,8,8,1024]{3,1,2,0:T(8,128)(2,1)S(1)} %get-tuple-element.26), kind=kOutput, calls=%fused_computation.9 | convolution fusion | flops 537133056 | bytes 9043968 | tf_op jit(solution)/shard_map/dot_general | solution.py:192
  79.5 4.9 %convolution_convert_fusion.3 = bf16[64,4096]{1,0:T(8,128)(2,1)S(1)} fusion(bf16[1024,4096]{1,0:T(8,128)(2,1)} %param.27, bf16[1,8,8,1024]{3,1,2,0:T(8,128)(2,1)S(1)} %get-tuple-element.25), kind=kOutput, calls=%fused_computation.10 | convolution fusion | flops 537133056 | bytes 9043968 | tf_op jit(solution)/shard_map/dot_general | solution.py:192
  93.6 6.1 %div.124 = f32[3,8,12,4096]{3,1,2,0:T(8,128)} reshape(f32[3,8,12,32,128]{4,3,1,2,0:T(8,128)} %div.123) | data formatting | bytes 9437184 | tf_op jit(solution)/shard_map/div | solution.py:171
  99.7 4.7 %all-to-all-done.1 = bf16[8,2,64,512]{3,2,1,0:T(8,128)(2,1)S(1)} async-done(((bf16[8,2,64,512]{3,2,1,0:T(8,128)(2,1)}), bf16[8,2,64,512]{3,2,1,0:T(8,128)(2,1)S(1)}, u32[]{:S(2)}, u32[]{:S(2)}) %all-to-all-start.1) | async-done | bytes 1048608 | tf_op jit(solution)/shard_map/all_to_all | solution.py:28
  110.0 6.4 %fusion.3 = bf16[8,3,12,4096]{3,0,2,1:T(8,128)(2,1)S(1)} fusion(f32[3,8,12,4096]{3,1,2,0:T(8,128)} %div.124, f32[1,8,12,4096]{3,1,2,0:T(8,128)S(1)} %bitcast.260, f32[1,8,12,4096]{3,1,2,0:T(8,128)} %bitcast.262, f32[1,8,12,4096]{3,1,2,0:T(8,128)} %bitcast.264), kind=kLoop, calls=%fused_computation.11 | loop fusion | flops 23592960 | bytes 11796480 | tf_op jit(solution)/shard_map/transpose | solution.py:174
  119.5 7.3 %all-to-all-start.6 = ((bf16[8,3,12,4096]{3,2,1,0:T(8,128)(2,1)}), bf16[8,3,12,4096]{3,2,1,0:T(8,128)(2,1)}, u32[]{:S(2)}, u32[]{:S(2)}) async-start(bf16[8,3,12,4096]{3,2,1,0:T(8,128)(2,1)} %copy.165), calls=%async_computation.6 | async-start | bytes 6291456 | tf_op jit(solution)/shard_map/all_to_all | solution.py:173
  127.1 44.2 %all-to-all-done.6 = bf16[8,3,12,4096]{3,2,1,0:T(8,128)(2,1)} async-done(((bf16[8,3,12,4096]{3,2,1,0:T(8,128)(2,1)}), bf16[8,3,12,4096]{3,2,1,0:T(8,128)(2,1)}, u32[]{:S(2)}, u32[]{:S(2)}) %all-to-all-start.6) | async-done | bytes 2359328 | tf_op jit(solution)/shard_map/all_to_all | solution.py:173
  183.9 8.7 %all-to-all-done.3 = bf16[16,8,4096]{2,1,0:T(8,128)(2,1)S(1)} async-done(((bf16[16,8,4096]{2,1,0:T(8,128)(2,1)}), bf16[16,8,4096]{2,1,0:T(8,128)(2,1)S(1)}, u32[]{:S(2)}, u32[]{:S(2)}) %all-to-all-start.3) | async-done | bytes 1048608 | tf_op jit(solution)/shard_map/all_to_all | solution.py:34
  200.4 16.4 %all-to-all-done.7 = bf16[16,8,4096]{2,1,0:T(8,128)(2,1)S(1)} async-done(((bf16[16,8,4096]{2,1,0:T(8,128)(2,1)}), bf16[16,8,4096]{2,1,0:T(8,128)(2,1)S(1)}, u32[]{:S(2)}, u32[]{:S(2)}) %all-to-all-start.7) | async-done | bytes 1048608 | tf_op jit(solution)/shard_map/all_to_all | solution.py:28
  217.0 10.1 %all_to_all.83 = bf16[8,8,512]{2,1,0:T(8,128)(2,1)S(1)} all-to-all(bf16[8,8,512]{2,1,0:T(8,128)(2,1)S(1)} %fusion.69), channel_id=1, replica_groups=mesh['fsdp'=16,'tp'=8] {'tp'}, dimensions={0} | all-to-all | bytes 131072 | tf_op jit(solution)/shard_map/all_to_all | solution.py:213
  227.6 10.3 %all_to_all.84 = bf16[8,8,512]{2,1,0:T(8,128)(2,1)S(1)} all-to-all(bf16[8,8,512]{2,1,0:T(8,128)(2,1)S(1)} %fusion.42), channel_id=1, replica_groups=mesh['fsdp'=16,'tp'=8] {'tp'}, dimensions={0} | all-to-all | bytes 131072 | tf_op jit(solution)/shard_map/all_to_all | solution.py:224
  238.2 19.1 %all_to_all.85 = bf16[16,8,4096]{2,1,0:T(8,128)(2,1)S(1)} all-to-all(bf16[16,8,4096]{2,1,0:T(8,128)(2,1)S(1)} %broadcast_in_dim.230), channel_id=1, replica_groups=mesh['fsdp'=16,'tp'=8] {'fsdp'}, dimensions={0} | all-to-all | bytes 2097152 | tf_op jit(solution)/shard_map/all_to_all | solution.py:34
  266.6 16.4 %all-to-all-done.11 = bf16[16,8,4096]{2,1,0:T(8,128)(2,1)S(1)} async-done(((bf16[16,8,4096]{2,1,0:T(8,128)(2,1)}), bf16[16,8,4096]{2,1,0:T(8,128)(2,1)S(1)}, u32[]{:S(2)}, u32[]{:S(2)}) %all-to-all-start.11) | async-done | bytes 1048608 | tf_op jit(solution)/shard_map/all_to_all | solution.py:28
  287.9 7.0 %all-to-all-done.12 = bf16[8,8,512]{2,1,0:T(8,128)(2,1)S(1)} async-done(((bf16[8,8,512]{2,1,0:T(8,128)(2,1)}), bf16[8,8,512]{2,1,0:T(8,128)(2,1)S(1)}, u32[]{:S(2)}, u32[]{:S(2)}) %all-to-all-start.12) | async-done | bytes 65568 | tf_op jit(solution)/shard_map/all_to_all | solution.py:213
  (144 shorter events, 64.9 us)
Async XLA Ops:
  0.6 12.7 %copy-start = (bf16[8,256,512]{2,1,0:T(8,128)(2,1)S(1)}, bf16[8,256,512]{2,1,0:T(8,128)(2,1)}, u32[]{:S(2)}) copy-start(bf16[8,256,512]{2,1,0:T(8,128)(2,1)} %param.16) | copy-start | bytes 6291460
  0.6 12.0 %copy-start.5 = (bf16[2,8,8192]{2,1,0:T(8,128)(2,1)S(1)}, bf16[2,8,8192]{2,1,0:T(8,128)(2,1)}, u32[]{:S(2)}) copy-start(bf16[2,8,8192]{2,1,0:T(8,128)(2,1)} %param.15) | copy-start | bytes 786436
  0.7 12.1 %copy-start.11 = (s32[8]{0:T(128)S(1)}, s32[8]{0:T(128)}, u32[]{:S(2)}) copy-start(s32[8]{0:T(128)} %param.20) | copy-start | bytes 100
  0.7 12.2 %copy-start.10 = (bf16[2,8,512]{2,1,0:T(8,128)(2,1)S(1)}, bf16[2,8,512]{2,1,0:T(8,128)(2,1)}, u32[]{:S(2)}) copy-start(bf16[2,8,512]{2,1,0:T(8,128)(2,1)} %param.18) | copy-start | bytes 49156
  5.7 25.9 %all-to-all-start.4 = ((f32[8,1,1536]{2,1,0:T(1,128)}), f32[8,1,1536]{2,1,0:T(1,128)S(1)}, u32[]{:S(2)}, u32[]{:S(2)}) async-start(f32[8,1,1536]{2,1,0:T(1,128)} %reshape.598), calls=%async_computation.4 | async-start | bytes 98304 | tf_op jit(solution)/shard_map/all_to_all | solution.py:34
  12.7 2.5 copy-start.9
  12.8 2.7 copy-start.12
  15.5 2.7 copy-start.7
  33.9 11.8 %all-to-all-start.5 = ((f32[16,1,1536]{2,1,0:T(1,128)}), f32[16,1,1536]{2,1,0:T(1,128)S(1)}, u32[]{:S(2)}, u32[]{:S(2)}) async-start(f32[16,1,1536]{2,1,0:T(1,128)} %reshape.600), calls=%async_computation.5 | async-start | bytes 196608 | tf_op jit(solution)/shard_map/all_to_all | solution.py:34
  45.8 16.6 %all-to-all-start = ((bf16[8,2,8192]{2,1,0:T(2,128)(2,1)}), bf16[8,2,8192]{2,1,0:T(2,128)(2,1)S(1)}, u32[]{:S(2)}, u32[]{:S(2)}) async-start(bf16[8,2,8192]{2,1,0:T(2,128)(2,1)} %reshape.602), calls=%async_computation | async-start | bytes 524288 | tf_op jit(solution)/shard_map/all_to_all | solution.py:189
  85.9 18.5 %all-to-all-start.1 = ((bf16[8,2,64,512]{3,2,1,0:T(8,128)(2,1)}), bf16[8,2,64,512]{3,2,1,0:T(8,128)(2,1)S(1)}, u32[]{:S(2)}, u32[]{:S(2)}) async-start(bf16[8,2,64,512]{3,2,1,0:T(8,128)(2,1)} %maximum_bitcast_fusion), calls=%async_computation.1 | async-start | bytes 2097152 | tf_op jit(solution)/shard_map/all_to_all | solution.py:28
  93.6 16.4 %copy-start.4 = (f32[8,12,4096]{2,0,1:T(8,128)S(1)}, f32[8,12,4096]{2,0,1:T(8,128)}, u32[]{:S(2)}) copy-start(f32[8,12,4096]{2,0,1:T(8,128)} %param.26) | copy-start | bytes 4718596
  106.2 13.3 %all-to-all-start.2 = ((bf16[8,8,512]{2,1,0:T(8,128)(2,1)}), bf16[8,8,512]{2,1,0:T(8,128)(2,1)S(1)}, u32[]{:S(2)}, u32[]{:S(2)}) async-start(bf16[8,8,512]{2,1,0:T(8,128)(2,1)} %fusion.41), calls=%async_computation.2 | async-start | bytes 131072 | tf_op jit(solution)/shard_map/all_to_all | solution.py:224
  119.5 7.5 %copy-start.6 = (f32[4096]{0:T(1024)S(1)}, f32[4096]{0:T(1024)}, u32[]{:S(2)}) copy-start(f32[4096]{0:T(1024)} %param.23) | copy-start | bytes 49156
  119.5 51.8 %all-to-all-start.6 = ((bf16[8,3,12,4096]{3,2,1,0:T(8,128)(2,1)}), bf16[8,3,12,4096]{3,2,1,0:T(8,128)(2,1)}, u32[]{:S(2)}, u32[]{:S(2)}) async-start(bf16[8,3,12,4096]{3,2,1,0:T(8,128)(2,1)} %copy.165), calls=%async_computation.6 | async-start | bytes 6291456 | tf_op jit(solution)/shard_map/all_to_all | solution.py:173
  172.4 20.2 %all-to-all-start.3 = ((bf16[16,8,4096]{2,1,0:T(8,128)(2,1)}), bf16[16,8,4096]{2,1,0:T(8,128)(2,1)S(1)}, u32[]{:S(2)}, u32[]{:S(2)}) async-start(bf16[16,8,4096]{2,1,0:T(8,128)(2,1)} %broadcast_in_dim.215), calls=%async_computation.3 | async-start | bytes 2097152 | tf_op jit(solution)/shard_map/all_to_all | solution.py:34
  179.7 16.9 %copy-start.2 = (bf16[96,4096]{1,0:T(8,128)(2,1)}, bf16[96,4096]{1,0:T(8,128)(2,1)S(1)}, u32[]{:S(2)}) copy-start(bf16[96,4096]{1,0:T(8,128)(2,1)S(1)} %reshape_squeeze.19) | copy-start | bytes 2359300
  181.4 15.2 %copy-start.3 = (bf16[96,4096]{1,0:T(8,128)(2,1)}, bf16[96,4096]{1,0:T(8,128)(2,1)S(1)}, u32[]{:S(2)}) copy-start(bf16[96,4096]{1,0:T(8,128)(2,1)S(1)} %reshape_squeeze.18) | copy-start | bytes 2359300
  183.9 16.4 %copy-start.8 = (f32[2,64,8]{1,2,0:T(8,128)S(1)}, f32[2,64,8]{1,2,0:T(8,128)}, u32[]{:S(2)}) copy-start(f32[2,64,8]{1,2,0:T(8,128)} %param.22) | copy-start | bytes 12292
  196.6 20.2 %all-to-all-start.7 = ((bf16[16,8,4096]{2,1,0:T(8,128)(2,1)}), bf16[16,8,4096]{2,1,0:T(8,128)(2,1)S(1)}, u32[]{:S(2)}, u32[]{:S(2)}) async-start(bf16[16,8,4096]{2,1,0:T(8,128)(2,1)} %fusion.1), calls=%async_computation.7 | async-start | bytes 2097152 | tf_op jit(solution)/shard_map/all_to_all | solution.py:28
  257.3 38.5 %copy-start.1 = (bf16[8,256,512]{2,1,0:T(8,128)(2,1)S(1)}, bf16[8,256,512]{2,1,0:T(8,128)(2,1)}, u32[]{:S(2)}) copy-start(bf16[8,256,512]{2,1,0:T(8,128)(2,1)} %param.16) | copy-start | bytes 6291460
  262.8 20.2 %all-to-all-start.11 = ((bf16[16,8,4096]{2,1,0:T(8,128)(2,1)}), bf16[16,8,4096]{2,1,0:T(8,128)(2,1)S(1)}, u32[]{:S(2)}, u32[]{:S(2)}) async-start(bf16[16,8,4096]{2,1,0:T(8,128)(2,1)} %fusion.2), calls=%async_computation.11 | async-start | bytes 2097152 | tf_op jit(solution)/shard_map/all_to_all | solution.py:28
  283.9 11.0 %all-to-all-start.12 = ((bf16[8,8,512]{2,1,0:T(8,128)(2,1)}), bf16[8,8,512]{2,1,0:T(8,128)(2,1)S(1)}, u32[]{:S(2)}, u32[]{:S(2)}) async-start(bf16[8,8,512]{2,1,0:T(8,128)(2,1)} %fusion.70), calls=%async_computation.12 | async-start | bytes 131072 | tf_op jit(solution)/shard_map/all_to_all | solution.py:213
where the time goes:
time: 297 us; the launch traced here: 296 us
  waiting for transfers between devices  111 us (37%)
  local copies, waits for them, and re-layouts  51.2 us (17%)
  starting transfers between devices  49.5 us (17%)
  blocking collectives  39.5 us (13%)
  matrix products  26.1 us (9%)
  other arithmetic  17 us (6%)
    all_to_all x1, waiting for transfers between devices, local(): lax.all_to_all(restored.transpose(1, 0, 2, 3), 'tp', split_axis=0, concat...  44.2 us
    all_to_all x3, waiting for transfers between devices, sent_and_summed(): lax.all_to_all(blocks, axis, split_axis=0, concat_axis=0, tiled=True)  37.5 us
    all_to_all x1, blocking collectives, copy_for_each(): lax.all_to_all(jnp.broadcast_to(array[None], (peers, *array.shape)), axis...  19.1 us
    all_to_all x3, starting transfers between devices, copy_for_each(): lax.all_to_all(jnp.broadcast_to(array[None], (peers, *array.shape)), axis...  16.2 us
    unnamed x38, local copies, waits for them, and re-layouts  15.3 us
    all_to_all x3, waiting for transfers between devices, copy_for_each(): lax.all_to_all(jnp.broadcast_to(array[None], (peers, *array.shape)), axis...  14.8 us
    all_to_all x3, starting transfers between devices, sent_and_summed(): lax.all_to_all(blocks, axis, split_axis=0, concat_axis=0, tiled=True)  11 us
    all_to_all x1, blocking collectives, collect_slots(): lax.all_to_all(chosen, 'tp', split_axis=0, concat_axis=0, tiled=True)  10.3 us
  transfers between devices with their start and end apart: 10, of which 8 were waited for; matrix products, arithmetic and copies ran while one was open for 16% of the time, Pallas kernels for 0%

commit v1 on v0

--- a/solution.py
+++ b/solution.py
@@ -186,7 +186,9 @@
             for s in range(2)
         ]
     )
-    regrouped = lax.all_to_all(heads, "tp", split_axis=2, concat_axis=1, tiled=True)
+    regrouped = jnp.concatenate(
+        lax.all_to_all(jnp.stack(jnp.split(heads, lax.axis_size("tp"), axis=2)), "tp", 0, 0), axis=1
+    )
     projections = []
     for s in range(2):
         projected = jnp.dot(regrouped[s], out_proj, preferred_element_type=jnp.float32)

time: 297 us -> 287 us (0.966)
  local copies, waits for them, and re-layouts: 51.2 us -> 37.2 us
  waiting for transfers between devices: 111 us -> 98.1 us
  other arithmetic: 17 us -> 26 us
  matrix products: 26.1 us -> 30.2 us
    all_to_all x3, waiting for transfers between devices: 37.5 us -> 29.5 us  [sent_and_summed(): lax.all_to_all(blocks, axis, split_axis=0, concat_axis=0, tiled=True)]
    another operation x3, local copies, waits for them, and re-layouts: 6.88 us -> 0.14 us  [local(): jnp.stack([attention_rows(queries[s], key_cache, value_cache, new_keys[:s...]
    unnamed x38 -> x62, local copies, waits for them, and re-layouts: 15.3 us -> 9.09 us
    all_to_all x1 -> x0, local copies, waits for them, and re-layouts: 5.94 us -> none  [local(): lax.all_to_all(heads, 'tp', split_axis=2, concat_axis=1, tiled=True)]
  transfers between devices with their start and end apart: 10 -> 10, of which waited for: 8 -> 8; matrix products, arithmetic and copies ran while one was open for 16% -> 18% of each run, Pallas kernels for 0% -> 0%
where the time goes in v1:
time: 287 us; the launch traced here: 285 us
  waiting for transfers between devices  98.1 us (34%)
  starting transfers between devices  52.2 us (18%)
  blocking collectives  39.5 us (14%)
  local copies, waits for them, and re-layouts  37.2 us (13%)
  matrix products  30.2 us (11%)
  other arithmetic  26 us (9%)
    all_to_all x1, waiting for transfers between devices, local(): lax.all_to_all(restored.transpose(1, 0, 2, 3), 'tp', split_axis=0, concat...  42.1 us
    all_to_all x3, waiting for transfers between devices, sent_and_summed(): lax.all_to_all(blocks, axis, split_axis=0, concat_axis=0, tiled=True)  29.5 us
    all_to_all x1, blocking collectives, copy_for_each(): lax.all_to_all(jnp.broadcast_to(array[None], (peers, *array.shape)), axis...  19.1 us
    all_to_all x3, starting transfers between devices, copy_for_each(): lax.all_to_all(jnp.broadcast_to(array[None], (peers, *array.shape)), axis...  16.2 us
    all_to_all x3, waiting for transfers between devices, copy_for_each(): lax.all_to_all(jnp.broadcast_to(array[None], (peers, *array.shape)), axis...  11.9 us
    all_to_all x3, starting transfers between devices, sent_and_summed(): lax.all_to_all(blocks, axis, split_axis=0, concat_axis=0, tiled=True)  10.9 us
    all_to_all x1, blocking collectives, collect_slots(): lax.all_to_all(chosen, 'tp', split_axis=0, concat_axis=0, tiled=True)  10.3 us
    all_to_all x1, blocking collectives, local(): lax.all_to_all(cut_along(weighted, 1, tp_count), 'tp', split_axis=0, conc...  10.1 us
  transfers between devices with their start and end apart: 10, of which 8 were waited for; matrix products, arithmetic and copies ran while one was open for 18% of the time, Pallas kernels for 0%

profile of v1, /device:TPU:0, one launch (start us, length us, event | category | flops | bytes accessed | tf_op | source)
XLA Modules:
  0.0 284.6 jit_solution(1923333466211442449)
XLA Ops:
  0.7 3.8 %fusion = f32[3,8,12,32]{1,3,2,0:T(8,128)S(1)} fusion(f32[1,8,12,32,128]{4,1,3,2,0:T(8,128)} %bitcast.284, f32[1,8,12,32,128]{4,1,3,2,0:T(8,128)} %bitcast.286, f32[1,8,12,32,128]{4,1,3,2,0:T(8,128)} %bitcast.288), kind=kLoop, calls=%fused_computation.4 | loop fusion | flops 4709376 | bytes 4755456 | tf_op jit(solution)/shard_map/reduce_max | solution.py:118
  5.7 7.0 %all-to-all-start.4 = ((f32[8,1,1536]{2,1,0:T(1,128)}), f32[8,1,1536]{2,1,0:T(1,128)S(1)}, u32[]{:S(2)}, u32[]{:S(2)}) async-start(f32[8,1,1536]{2,1,0:T(1,128)} %reshape.603), calls=%async_computation.4 | async-start | bytes 98304 | tf_op jit(solution)/shard_map/all_to_all | solution.py:34
  26.8 5.5 %all-to-all-start.5 = ((f32[16,1,1536]{2,1,0:T(1,128)}), f32[16,1,1536]{2,1,0:T(1,128)S(1)}, u32[]{:S(2)}, u32[]{:S(2)}) async-start(f32[16,1,1536]{2,1,0:T(1,128)} %reshape.605), calls=%async_computation.5 | async-start | bytes 196608 | tf_op jit(solution)/shard_map/all_to_all | solution.py:34
  33.2 5.5 %all-to-all-done.5 = f32[16,1,1536]{2,1,0:T(1,128)S(1)} async-done(((f32[16,1,1536]{2,1,0:T(1,128)}), f32[16,1,1536]{2,1,0:T(1,128)S(1)}, u32[]{:S(2)}, u32[]{:S(2)}) %all-to-all-start.5) | async-done | bytes 98336 | tf_op jit(solution)/shard_map/all_to_all | solution.py:34
  38.7 7.8 %all-to-all-start = ((bf16[8,2,8,1024]{3,2,1,0:T(8,128)(2,1)}), bf16[8,2,8,1024]{3,2,1,0:T(8,128)(2,1)S(1)}, u32[]{:S(2)}, u32[]{:S(2)}) async-start(bf16[8,2,8,1024]{3,2,1,0:T(8,128)(2,1)} %constant_dynamic-update-slice_fusion.2), calls=%async_computation | async-start | bytes 524288 | tf_op jit(solution)/shard_map/all_to_all | solution.py:190
  47.6 7.6 %all-to-all-done = bf16[8,2,8,1024]{3,2,1,0:T(8,128)(2,1)S(1)} async-done(((bf16[8,2,8,1024]{3,2,1,0:T(8,128)(2,1)}), bf16[8,2,8,1024]{3,2,1,0:T(8,128)(2,1)S(1)}, u32[]{:S(2)}, u32[]{:S(2)}) %all-to-all-start) | async-done | bytes 262176 | tf_op jit(solution)/shard_map/all_to_all | solution.py:190
  55.3 4.9 %convolution_convert_fusion.2 = bf16[64,4096]{1,0:T(8,128)(2,1)S(1)} fusion(bf16[1024,4096]{1,0:T(8,128)(2,1)} %param.27, bf16[2,8,8,1024]{3,2,0,1:T(8,128)(2,1)S(1)} %bitcast.294), kind=kOutput, calls=%fused_computation.9 | convolution fusion | flops 537133056 | bytes 9043968 | tf_op jit(solution)/shard_map/dot_general | solution.py:194
  60.2 5.0 %convolution_convert_fusion.3 = bf16[64,4096]{1,0:T(8,128)(2,1)S(1)} fusion(bf16[1024,4096]{1,0:T(8,128)(2,1)} %param.27, bf16[2,8,8,1024]{3,2,0,1:T(8,128)(2,1)S(1)} %bitcast.295), kind=kOutput, calls=%fused_computation.10 | convolution fusion | flops 537133056 | bytes 9043968 | tf_op jit(solution)/shard_map/dot_general | solution.py:194
  79.0 6.0 %div.124 = f32[3,8,12,4096]{3,1,2,0:T(8,128)} reshape(f32[3,8,12,32,128]{4,3,1,2,0:T(8,128)} %div.123) | data formatting | bytes 9437184 | tf_op jit(solution)/shard_map/div | solution.py:171
  88.6 6.7 %all-to-all-start.2 = ((bf16[8,8,512]{2,1,0:T(8,128)(2,1)}), bf16[8,8,512]{2,1,0:T(8,128)(2,1)S(1)}, u32[]{:S(2)}, u32[]{:S(2)}) async-start(bf16[8,8,512]{2,1,0:T(8,128)(2,1)} %fusion.41), calls=%async_computation.2 | async-start | bytes 131072 | tf_op jit(solution)/shard_map/all_to_all | solution.py:226
  95.3 6.6 %fusion.3 = bf16[8,3,12,4096]{3,0,2,1:T(8,128)(2,1)S(1)} fusion(f32[3,8,12,4096]{3,1,2,0:T(8,128)} %div.124, f32[1,8,12,4096]{3,1,2,0:T(8,128)} %bitcast.285, f32[1,8,12,4096]{3,1,2,0:T(8,128)} %bitcast.287, f32[1,8,12,4096]{3,1,2,0:T(8,128)} %bitcast.289), kind=kLoop, calls=%fused_computation.11 | loop fusion | flops 23592960 | bytes 11796480 | tf_op jit(solution)/shard_map/transpose | solution.py:174
  105.0 7.3 %all-to-all-start.6 = ((bf16[8,3,12,4096]{3,2,1,0:T(8,128)(2,1)}), bf16[8,3,12,4096]{3,2,1,0:T(8,128)(2,1)}, u32[]{:S(2)}, u32[]{:S(2)}) async-start(bf16[8,3,12,4096]{3,2,1,0:T(8,128)(2,1)} %copy.129), calls=%async_computation.6 | async-start | bytes 6291456 | tf_op jit(solution)/shard_map/all_to_all | solution.py:173
  112.6 42.1 %all-to-all-done.6 = bf16[8,3,12,4096]{3,2,1,0:T(8,128)(2,1)} async-done(((bf16[8,3,12,4096]{3,2,1,0:T(8,128)(2,1)}), bf16[8,3,12,4096]{3,2,1,0:T(8,128)(2,1)}, u32[]{:S(2)}, u32[]{:S(2)}) %all-to-all-start.6) | async-done | bytes 2359328 | tf_op jit(solution)/shard_map/all_to_all | solution.py:173
  169.6 6.4 %all-to-all-done.3 = bf16[16,8,4096]{2,1,0:T(8,128)(2,1)S(1)} async-done(((bf16[16,8,4096]{2,1,0:T(8,128)(2,1)}), bf16[16,8,4096]{2,1,0:T(8,128)(2,1)S(1)}, u32[]{:S(2)}, u32[]{:S(2)}) %all-to-all-start.3) | async-done | bytes 1048608 | tf_op jit(solution)/shard_map/all_to_all | solution.py:34
  178.2 3.8 %fusion.1 = bf16[16,8,4096]{2,1,0:T(8,128)(2,1)} fusion(bf16[96,4096]{1,0:T(8,128)(2,1)} %reshape_squeeze.19, bf16[96,4096]{1,0:T(8,128)(2,1)} %reshape_squeeze.18, bf16[16,8,4096]{2,1,0:T(8,128)(2,1)S(1)} %all-to-all-done.3, f32[128,96]{0,1:T(8,128)} %fusion.51), kind=kOutput, calls=%fused_computation.7 | convolution fusion | flops 201924608 | bytes 3719168 | tf_op jit(solution)/shard_map/dot_general | solution.py:211
  182.0 3.7 %all-to-all-start.7 = ((bf16[16,8,4096]{2,1,0:T(8,128)(2,1)}), bf16[16,8,4096]{2,1,0:T(8,128)(2,1)S(1)}, u32[]{:S(2)}, u32[]{:S(2)}) async-start(bf16[16,8,4096]{2,1,0:T(8,128)(2,1)} %fusion.1), calls=%async_computation.7 | async-start | bytes 2097152 | tf_op jit(solution)/shard_map/all_to_all | solution.py:28
  189.5 12.6 %all-to-all-done.7 = bf16[16,8,4096]{2,1,0:T(8,128)(2,1)S(1)} async-done(((bf16[16,8,4096]{2,1,0:T(8,128)(2,1)}), bf16[16,8,4096]{2,1,0:T(8,128)(2,1)S(1)}, u32[]{:S(2)}, u32[]{:S(2)}) %all-to-all-start.7) | async-done | bytes 1048608 | tf_op jit(solution)/shard_map/all_to_all | solution.py:28
  203.0 10.1 %all_to_all.73 = bf16[8,8,512]{2,1,0:T(8,128)(2,1)S(1)} all-to-all(bf16[8,8,512]{2,1,0:T(8,128)(2,1)S(1)} %fusion.65), channel_id=1, replica_groups=mesh['fsdp'=16,'tp'=8] {'tp'}, dimensions={0} | all-to-all | bytes 131072 | tf_op jit(solution)/shard_map/all_to_all | solution.py:215
  215.7 10.3 %all_to_all.74 = bf16[8,8,512]{2,1,0:T(8,128)(2,1)S(1)} all-to-all(bf16[8,8,512]{2,1,0:T(8,128)(2,1)S(1)} %fusion.42), channel_id=1, replica_groups=mesh['fsdp'=16,'tp'=8] {'tp'}, dimensions={0} | all-to-all | bytes 131072 | tf_op jit(solution)/shard_map/all_to_all | solution.py:226
  227.1 19.1 %all_to_all.75 = bf16[16,8,4096]{2,1,0:T(8,128)(2,1)S(1)} all-to-all(bf16[16,8,4096]{2,1,0:T(8,128)(2,1)S(1)} %broadcast_in_dim.230), channel_id=1, replica_groups=mesh['fsdp'=16,'tp'=8] {'fsdp'}, dimensions={0} | all-to-all | bytes 2097152 | tf_op jit(solution)/shard_map/all_to_all | solution.py:34
  247.9 3.8 %fusion.2 = bf16[16,8,4096]{2,1,0:T(8,128)(2,1)} fusion(bf16[96,4096]{1,0:T(8,128)(2,1)} %reshape_squeeze.19, bf16[96,4096]{1,0:T(8,128)(2,1)} %reshape_squeeze.18, bf16[16,8,4096]{2,1,0:T(8,128)(2,1)S(1)} %all_to_all.75, f32[128,96]{0,1:T(8,128)S(1)} %fusion.47), kind=kOutput, calls=%fused_computation.8 | convolution fusion | flops 201924608 | bytes 3719168 | tf_op jit(solution)/shard_map/dot_general | solution.py:211
  251.6 3.7 %all-to-all-start.11 = ((bf16[16,8,4096]{2,1,0:T(8,128)(2,1)}), bf16[16,8,4096]{2,1,0:T(8,128)(2,1)S(1)}, u32[]{:S(2)}, u32[]{:S(2)}) async-start(bf16[16,8,4096]{2,1,0:T(8,128)(2,1)} %fusion.2), calls=%async_computation.11 | async-start | bytes 2097152 | tf_op jit(solution)/shard_map/all_to_all | solution.py:28
  255.5 16.4 %all-to-all-done.11 = bf16[16,8,4096]{2,1,0:T(8,128)(2,1)S(1)} async-done(((bf16[16,8,4096]{2,1,0:T(8,128)(2,1)}), bf16[16,8,4096]{2,1,0:T(8,128)(2,1)S(1)}, u32[]{:S(2)}, u32[]{:S(2)}) %all-to-all-start.11) | async-done | bytes 1048608 | tf_op jit(solution)/shard_map/all_to_all | solution.py:28
  276.7 7.0 %all-to-all-done.12 = bf16[8,8,512]{2,1,0:T(8,128)(2,1)S(1)} async-done(((bf16[8,8,512]{2,1,0:T(8,128)(2,1)}), bf16[8,8,512]{2,1,0:T(8,128)(2,1)S(1)}, u32[]{:S(2)}, u32[]{:S(2)}) %all-to-all-start.12) | async-done | bytes 65568 | tf_op jit(solution)/shard_map/all_to_all | solution.py:215
  (166 shorter events, 70.5 us)
Async XLA Ops:
  0.6 12.2 %copy-start = (bf16[8,256,512]{2,1,0:T(8,128)(2,1)S(1)}, bf16[8,256,512]{2,1,0:T(8,128)(2,1)}, u32[]{:S(2)}) copy-start(bf16[8,256,512]{2,1,0:T(8,128)(2,1)} %param.16) | copy-start | bytes 6291460
  0.7 4.1 %copy-start.18 = (pred[12]{0:T(512)(128)(4,1)}, pred[12]{0:T(512)(128)(4,1)S(1)}, u32[]{:S(2)}) copy-start(pred[12]{0:T(512)(128)(4,1)S(1)} %subtract_compare_fusion) | copy-start | bytes 40
  0.7 12.0 %copy-start.4 = (bf16[2,8,8192]{2,1,0:T(8,128)(2,1)S(1)}, bf16[2,8,8192]{2,1,0:T(8,128)(2,1)}, u32[]{:S(2)}) copy-start(bf16[2,8,8192]{2,1,0:T(8,128)(2,1)} %param.15) | copy-start | bytes 786436
  0.7 12.1 %copy-start.17 = (bf16[2,8,512]{2,1,0:T(8,128)(2,1)S(1)}, bf16[2,8,512]{2,1,0:T(8,128)(2,1)}, u32[]{:S(2)}) copy-start(bf16[2,8,512]{2,1,0:T(8,128)(2,1)} %param.18) | copy-start | bytes 49156
  4.5 9.1 %copy-start.20 = (s32[8]{0:T(128)S(1)}, s32[8]{0:T(128)}, u32[]{:S(2)}) copy-start(s32[8]{0:T(128)} %param.20) | copy-start | bytes 100
  5.7 18.8 %all-to-all-start.4 = ((f32[8,1,1536]{2,1,0:T(1,128)}), f32[8,1,1536]{2,1,0:T(1,128)S(1)}, u32[]{:S(2)}, u32[]{:S(2)}) async-start(f32[8,1,1536]{2,1,0:T(1,128)} %reshape.603), calls=%async_computation.4 | async-start | bytes 98304 | tf_op jit(solution)/shard_map/all_to_all | solution.py:34
  16.0 7.3 %copy-start.15 = (s32[2,64,8]{1,2,0:T(8,128)S(1)}, s32[2,64,8]{1,2,0:T(8,128)}, u32[]{:S(2)}) copy-start(s32[2,64,8]{1,2,0:T(8,128)} %param.21) | copy-start | bytes 12292
  26.8 11.8 %all-to-all-start.5 = ((f32[16,1,1536]{2,1,0:T(1,128)}), f32[16,1,1536]{2,1,0:T(1,128)S(1)}, u32[]{:S(2)}, u32[]{:S(2)}) async-start(f32[16,1,1536]{2,1,0:T(1,128)} %reshape.605), calls=%async_computation.5 | async-start | bytes 196608 | tf_op jit(solution)/shard_map/all_to_all | solution.py:34
  38.7 16.6 %all-to-all-start = ((bf16[8,2,8,1024]{3,2,1,0:T(8,128)(2,1)}), bf16[8,2,8,1024]{3,2,1,0:T(8,128)(2,1)S(1)}, u32[]{:S(2)}, u32[]{:S(2)}) async-start(bf16[8,2,8,1024]{3,2,1,0:T(8,128)(2,1)} %constant_dynamic-update-slice_fusion.2), calls=%async_computation | async-start | bytes 524288 | tf_op jit(solution)/shard_map/all_to_all | solution.py:190
  47.6 12.6 %copy-start.5 = (f32[3,8,12,32]{3,1,0,2:T(8,128)}, f32[3,8,12,32]{3,1,0,2:T(8,128)S(1)}, u32[]{:S(2)}) copy-start(f32[3,8,12,32]{3,1,0,2:T(8,128)S(1)} %constant_dynamic-update-slice_fusion.12) | copy-start | bytes 110596
  67.0 18.5 %all-to-all-start.1 = ((bf16[8,2,64,512]{3,2,1,0:T(8,128)(2,1)}), bf16[8,2,64,512]{3,2,1,0:T(8,128)(2,1)S(1)}, u32[]{:S(2)}, u32[]{:S(2)}) async-start(bf16[8,2,64,512]{3,2,1,0:T(8,128)(2,1)} %maximum_bitcast_fusion), calls=%async_computation.1 | async-start | bytes 2097152 | tf_op jit(solution)/shard_map/all_to_all | solution.py:28
  88.6 16.4 %all-to-all-start.2 = ((bf16[8,8,512]{2,1,0:T(8,128)(2,1)}), bf16[8,8,512]{2,1,0:T(8,128)(2,1)S(1)}, u32[]{:S(2)}, u32[]{:S(2)}) async-start(bf16[8,8,512]{2,1,0:T(8,128)(2,1)} %fusion.41), calls=%async_computation.2 | async-start | bytes 131072 | tf_op jit(solution)/shard_map/all_to_all | solution.py:226
  105.0 7.5 %copy-start.7 = (f32[4096]{0:T(1024)S(1)}, f32[4096]{0:T(1024)}, u32[]{:S(2)}) copy-start(f32[4096]{0:T(1024)} %param.23) | copy-start | bytes 49156
  105.0 49.7 %all-to-all-start.6 = ((bf16[8,3,12,4096]{3,2,1,0:T(8,128)(2,1)}), bf16[8,3,12,4096]{3,2,1,0:T(8,128)(2,1)}, u32[]{:S(2)}, u32[]{:S(2)}) async-start(bf16[8,3,12,4096]{3,2,1,0:T(8,128)(2,1)} %copy.129), calls=%async_computation.6 | async-start | bytes 6291456 | tf_op jit(solution)/shard_map/all_to_all | solution.py:173
  155.7 20.2 %all-to-all-start.3 = ((bf16[16,8,4096]{2,1,0:T(8,128)(2,1)}), bf16[16,8,4096]{2,1,0:T(8,128)(2,1)S(1)}, u32[]{:S(2)}, u32[]{:S(2)}) async-start(bf16[16,8,4096]{2,1,0:T(8,128)(2,1)} %broadcast_in_dim.215), calls=%async_computation.3 | async-start | bytes 2097152 | tf_op jit(solution)/shard_map/all_to_all | solution.py:34
  182.0 20.2 %all-to-all-start.7 = ((bf16[16,8,4096]{2,1,0:T(8,128)(2,1)}), bf16[16,8,4096]{2,1,0:T(8,128)(2,1)S(1)}, u32[]{:S(2)}, u32[]{:S(2)}) async-start(bf16[16,8,4096]{2,1,0:T(8,128)(2,1)} %fusion.1), calls=%async_computation.7 | async-start | bytes 2097152 | tf_op jit(solution)/shard_map/all_to_all | solution.py:28
  247.8 7.5 %copy-start.9 = (s32[64,8]{0,1:T(8,128)S(1)}, s32[64,8]{0,1:T(8,128)}, u32[]{:S(2)}) copy-start(s32[64,8]{0,1:T(8,128)} %copy-done.8) | copy-start | bytes 6148
  247.8 7.5 %copy-start.14 = (f32[64,8]{0,1:T(8,128)S(1)}, f32[64,8]{0,1:T(8,128)}, u32[]{:S(2)}) copy-start(f32[64,8]{0,1:T(8,128)} %get-tuple-element.33) | copy-start | bytes 6148
  247.8 7.5 %copy-start.19 = (f32[64]{0:T(128)S(1)}, f32[64]{0:T(128)}, u32[]{:S(2)}) copy-start(f32[64]{0:T(128)} %get-tuple-element.14) | copy-start | bytes 772
  247.8 7.5 %copy-start.6 = (s32[8,64]{1,0:T(8,128)S(1)}, s32[8,64]{1,0:T(8,128)}, u32[]{:S(2)}) copy-start(s32[8,64]{1,0:T(8,128)} %get-tuple-element.16) | copy-start | bytes 6148
  247.8 7.5 %copy-start.12 = (pred[8,64]{1,0:T(8,128)(4,1)S(1)}, pred[8,64]{1,0:T(8,128)(4,1)}, u32[]{:S(2)}) copy-start(pred[8,64]{1,0:T(8,128)(4,1)} %copy-done.11) | copy-start | bytes 1540
  247.9 35.9 %copy-start.2 = (bf16[64,512]{1,0:T(8,128)(2,1)S(1)}, bf16[64,512]{1,0:T(8,128)(2,1)}, u32[]{:S(2)}) copy-start(bf16[64,512]{1,0:T(8,128)(2,1)} %copy-done.1) | copy-start | bytes 196612
  251.6 20.2 %all-to-all-start.11 = ((bf16[16,8,4096]{2,1,0:T(8,128)(2,1)}), bf16[16,8,4096]{2,1,0:T(8,128)(2,1)S(1)}, u32[]{:S(2)}, u32[]{:S(2)}) async-start(bf16[16,8,4096]{2,1,0:T(8,128)(2,1)} %fusion.2), calls=%async_computation.11 | async-start | bytes 2097152 | tf_op jit(solution)/shard_map/all_to_all | solution.py:28
  272.7 11.0 %all-to-all-start.12 = ((bf16[8,8,512]{2,1,0:T(8,128)(2,1)}), bf16[8,8,512]{2,1,0:T(8,128)(2,1)S(1)}, u32[]{:S(2)}, u32[]{:S(2)}) async-start(bf16[8,8,512]{2,1,0:T(8,128)(2,1)} %fusion.66), calls=%async_computation.12 | async-start | bytes 131072 | tf_op jit(solution)/shard_map/all_to_all | solution.py:215
  (8 other events, 8.5 us)
